TPU v7x, 256 devices: a whole 4x4x8 slice. The times are simulated.
256 devices in a mesh: rows: 8 (over y, core), cols: 32 (over z, x).
Axes of the slice: x: 4, y: 4, z: 8, core: 2. Of those that a mesh axis runs over, the one named last changes fastest.
Arguments:
- noise: bfloat16 [32768, 256], P(('rows', 'cols')), may hold values from -24 to 24
- data: bfloat16 [32768, 256], P(('cols', 'rows')), may hold values from -6 to 6
Outputs:
- targets: float32 [32768, 256], P(('rows', 'cols'))
All inputs are finite; a program needn't handle non-finite values.
Results may differ from a plain program's by a relative error of at most 0.00055.
Values may be sent and summed in bfloat16 or wider, within the bound.
A program may use at most 128 MiB of HBM per device.

v0:
```python
import math

import jax
import jax.numpy as jnp
from jax import lax
from jax.sharding import PartitionSpec as P

ITERS = 4


EPS = 0.5
INV_EPS = 2.0


def similarity(left, right, scale):
    return (
        lax.dot_general(left, right, (((1,), (1,)), ((), ())), preferred_element_type=jnp.float32)
        * scale
    )


def per_device(noise, data):
    rows_here = lax.all_gather(noise, "cols", axis=0, tiled=True)
    cols_here = lax.all_gather(data, "rows", axis=0, tiled=True)
    scale = noise.shape[1] ** (-0.5)
    log_a = -math.log(rows_here.shape[0] * lax.axis_size("rows"))
    log_b = -math.log(cols_here.shape[0] * lax.axis_size("cols"))
    tile = similarity(rows_here, cols_here, scale)
    g_vec = jnp.zeros((cols_here.shape[0],), jnp.float32)
    for step_index in range(ITERS):
        z_rows = (g_vec[None, :] + tile) * INV_EPS
        top = lax.pmax(jnp.max(z_rows, 1), "cols")
        total = lax.psum(jnp.sum(jnp.exp(z_rows - top[:, None]), 1), "cols")
        f_vec = EPS * (log_a - top - jnp.log(total))
        z_cols = (f_vec[:, None] + tile) * INV_EPS
        col_top = lax.pmax(jnp.max(z_cols, 0), "rows")
        col_total = lax.psum(jnp.sum(jnp.exp(z_cols - col_top[None, :]), 0), "rows")
        g_vec = EPS * (log_b - col_top - jnp.log(col_total))
    z_final = (g_vec[None, :] + tile) * INV_EPS
    top = lax.pmax(jnp.max(z_final, 1), "cols")
    weights = jnp.exp(z_final - top[:, None]).astype(jnp.bfloat16)
    numerator = jnp.dot(weights, cols_here, preferred_element_type=jnp.float32)
    denominator = jnp.sum(weights.astype(jnp.float32), 1)
    numerator, denominator = (
        lax.psum_scatter(numerator, "cols", scatter_dimension=0, tiled=True),
        lax.psum_scatter(denominator, "cols", scatter_dimension=0, tiled=True),
    )
    return numerator / denominator[:, None]


def solution(mesh):
    in_specs = (P(("rows", "cols"), None), P(("cols", "rows"), None))
    out_specs = P(("rows", "cols"), None)
    return jax.shard_map(
        per_device, mesh=mesh, in_specs=in_specs, out_specs=out_specs, check_vma=False
    )
```

profile of v0, /device:TPU:1, one launch (start us, length us, event | category | flops | bytes accessed | tf_op | source)
XLA Modules:
  0.0 1805.2 jit_solution(7146339016023826758)
XLA Ops:
  6.5 0.0 all-gather.2.cloned.1.call-start
  6.5 0.7 all-gather.2.cloned.1.call-update
  7.3 0.0 reduce-scatter.2.cloned.1.call-start
  7.3 16.4 all_gather.7
  23.7 64.1 %all-gather.2.cloned.1.call-done = bf16[4096,256]{1,0:T(8,128)(2,1)} async-done(((bf16[128,256]{1,0:T(8,128)(2,1)}), bf16[4096,256]{1,0:T(8,128)(2,1)}) %all-gather.2.cloned.1.call-update) | async-done | bytes 2097168 | tf_op jit(solution)/shard_map/all_gather | solution.py:23
  87.8 9.7 multiply_reduce_fusion
  97.4 112.6 %pmax.63 = f32[4096]{0:T(1024)S(1)} all-reduce(f32[4096]{0:T(1024)S(1)} %get-tuple-element.7), channel_id=1, replica_groups=mesh['rows'=8,'cols'=32] {'cols'}, use_global_device_ids=true, to_apply=%region_1.0 | all-reduce | flops 4096 | bytes 32768 | tf_op jit(solution)/shard_map/pmax | solution.py:32
  210.0 8.5 exponential_reduce_fusion.7
  218.5 110.5 %psum.56 = f32[4096]{0:T(1024)S(1)} all-reduce(f32[4096]{0:T(1024)S(1)} %exponential_reduce_fusion.7), channel_id=1, replica_groups=mesh['rows'=8,'cols'=32] {'cols'}, use_global_device_ids=true, to_apply=%region_3.0 | all-reduce | flops 4096 | bytes 32768 | tf_op jit(solution)/shard_map/psum | solution.py:33
  329.1 8.0 fusion
  337.1 71.0 %pmax.64 = f32[1024]{0:T(1024)S(1)} all-reduce(f32[1024]{0:T(1024)S(1)} %fusion), channel_id=1, replica_groups=mesh['rows'=8,'cols'=32] {'rows'}, use_global_device_ids=true, to_apply=%region_5.0 | all-reduce | flops 1024 | bytes 8192 | tf_op jit(solution)/shard_map/pmax | solution.py:36
  408.0 8.1 exponential_reduce_fusion.6
  416.1 12.9 psum.57
  429.0 8.2 fusion.1
  437.2 109.9 %pmax.65 = f32[4096]{0:T(1024)S(1)} all-reduce(f32[4096]{0:T(1024)S(1)} %fusion.1), channel_id=1, replica_groups=mesh['rows'=8,'cols'=32] {'cols'}, use_global_device_ids=true, to_apply=%region_9.0 | all-reduce | flops 4096 | bytes 32768 | tf_op jit(solution)/shard_map/pmax | solution.py:32
  547.0 8.0 exponential_reduce_fusion.5
  555.1 110.3 %psum.58 = f32[4096]{0:T(1024)S(1)} all-reduce(f32[4096]{0:T(1024)S(1)} %exponential_reduce_fusion.5), channel_id=1, replica_groups=mesh['rows'=8,'cols'=32] {'cols'}, use_global_device_ids=true, to_apply=%region_11.0 | all-reduce | flops 4096 | bytes 32768 | tf_op jit(solution)/shard_map/psum | solution.py:33
  665.4 8.0 fusion.2
  673.4 67.6 %pmax.66 = f32[1024]{0:T(1024)S(1)} all-reduce(f32[1024]{0:T(1024)S(1)} %fusion.2), channel_id=1, replica_groups=mesh['rows'=8,'cols'=32] {'rows'}, use_global_device_ids=true, to_apply=%region_13.0 | all-reduce | flops 1024 | bytes 8192 | tf_op jit(solution)/shard_map/pmax | solution.py:36
  741.0 8.1 exponential_reduce_fusion.4
  749.1 12.4 psum.59
  761.5 8.2 fusion.3
  769.7 109.9 %pmax.67 = f32[4096]{0:T(1024)S(1)} all-reduce(f32[4096]{0:T(1024)S(1)} %fusion.3), channel_id=1, replica_groups=mesh['rows'=8,'cols'=32] {'cols'}, use_global_device_ids=true, to_apply=%region_17.0 | all-reduce | flops 4096 | bytes 32768 | tf_op jit(solution)/shard_map/pmax | solution.py:32
  879.5 8.0 exponential_reduce_fusion.3
  887.6 110.5 %psum.60 = f32[4096]{0:T(1024)S(1)} all-reduce(f32[4096]{0:T(1024)S(1)} %exponential_reduce_fusion.3), channel_id=1, replica_groups=mesh['rows'=8,'cols'=32] {'cols'}, use_global_device_ids=true, to_apply=%region_19.0 | all-reduce | flops 4096 | bytes 32768 | tf_op jit(solution)/shard_map/psum | solution.py:33
  998.1 8.0 fusion.4
  1006.1 67.6 %pmax.68 = f32[1024]{0:T(1024)S(1)} all-reduce(f32[1024]{0:T(1024)S(1)} %fusion.4), channel_id=1, replica_groups=mesh['rows'=8,'cols'=32] {'rows'}, use_global_device_ids=true, to_apply=%region_21.0 | all-reduce | flops 1024 | bytes 8192 | tf_op jit(solution)/shard_map/pmax | solution.py:36
  1073.7 8.1 exponential_reduce_fusion.2
  1081.7 12.4 psum.61
  1094.2 8.2 fusion.5
  1102.3 109.9 %pmax.69 = f32[4096]{0:T(1024)S(1)} all-reduce(f32[4096]{0:T(1024)S(1)} %fusion.5), channel_id=1, replica_groups=mesh['rows'=8,'cols'=32] {'cols'}, use_global_device_ids=true, to_apply=%region_25.0 | all-reduce | flops 4096 | bytes 32768 | tf_op jit(solution)/shard_map/pmax | solution.py:32
  1212.2 8.0 exponential_reduce_fusion.1
  1220.2 110.3 %psum.62 = f32[4096]{0:T(1024)S(1)} all-reduce(f32[4096]{0:T(1024)S(1)} %exponential_reduce_fusion.1), channel_id=1, replica_groups=mesh['rows'=8,'cols'=32] {'cols'}, use_global_device_ids=true, to_apply=%region_27.0 | all-reduce | flops 4096 | bytes 32768 | tf_op jit(solution)/shard_map/psum | solution.py:33
  1330.5 8.0 fusion.6
  1338.6 67.6 %pmax.70 = f32[1024]{0:T(1024)S(1)} all-reduce(f32[1024]{0:T(1024)S(1)} %fusion.6), channel_id=1, replica_groups=mesh['rows'=8,'cols'=32] {'rows'}, use_global_device_ids=true, to_apply=%region_29.0 | all-reduce | flops 1024 | bytes 8192 | tf_op jit(solution)/shard_map/pmax | solution.py:36
  1406.1 8.1 exponential_reduce_fusion
  1414.2 12.6 psum.63
  1426.9 8.2 fusion.7
  1435.0 109.9 %pmax.71 = f32[4096]{0:T(1024)S(1)} all-reduce(f32[4096]{0:T(1024)S(1)} %fusion.7), channel_id=1, replica_groups=mesh['rows'=8,'cols'=32] {'cols'}, use_global_device_ids=true, to_apply=%region_33.0 | all-reduce | flops 4096 | bytes 32768 | tf_op jit(solution)/shard_map/pmax | solution.py:40
  1544.9 8.2 convert_reduce_fusion
  1553.1 0.0 copy-start
  1553.1 4.4 fusion.8
  1557.5 0.0 reduce-scatter.2.cloned.1.call-update
  1557.5 0.0 copy-done
  1557.5 0.6 dynamic-slice
  1558.8 110.4 %all-reduce = f32[4096]{0:T(1024)S(1)} all-reduce(f32[4096]{0:T(1024)S(1)} %get-tuple-element.5), channel_id=3, replica_groups=mesh['rows'=8,'cols'=32] {'cols'}, use_global_device_ids=true, to_apply=%region_36.0.clone | all-reduce | flops 4096 | bytes 32768
  1669.2 0.1 dynamic-slice.1
  1669.2 127.2 %reduce-scatter.2.cloned.1.call-done = f32[128,256]{1,0:T(8,128)} async-done(((f32[4096,256]{1,0:T(8,128)}), f32[128,256]{1,0:T(8,128)}) %reduce-scatter.2.cloned.1.call-update) | async-done | bytes 131088 | tf_op jit(solution)/shard_map/reduce_scatter | solution.py:45
  1796.5 1.6 broadcast_divide_fusion
  (8 shorter events, 0.1 us)
Async XLA Ops:
  6.5 81.2 %all-gather.2.cloned.1.call-start = ((), (), s32[]{:S(2)}) async-start(), calls=%async_computation.1 | async-start | bytes 2162688 | tf_op jit(solution)/shard_map/all_gather | solution.py:23
  7.3 1789.2 %reduce-scatter.2.cloned.1.call-start = ((), (), s32[]{:S(2)}) async-start(), calls=%async_computation.2 | async-start | bytes 4325376 | tf_op jit(solution)/shard_map/reduce_scatter | solution.py:45
  1553.1 4.4 copy-start
Sparse Core Ops, SparseCore 0:
  9.9 77.7 all-gather.1
  1557.7 238.7 reduce-scatter.1
where the time goes:
time: 1820 us; the launch traced here: 1810 us
  blocking collectives  1440 us (79%)
  waiting for transfers between devices  192 us (11%)
  other arithmetic  139 us (8%)
    pmax x4, blocking collectives, per_device(): top = lax.pmax(jnp.max(z_rows, 1), 'cols')  442 us
    psum x4, blocking collectives, per_device(): total = lax.psum(jnp.sum(jnp.exp(z_rows - top[:, None]), 1), 'cols')  442 us
    pmax x4, blocking collectives, per_device(): col_top = lax.pmax(jnp.max(z_cols, 0), 'rows')  274 us
    reduce_scatter x1, waiting for transfers between devices, per_device(): lax.psum_scatter(numerator, 'cols', scatter_dimension=0, tiled=True)  127 us
    unnamed x1, blocking collectives  110 us
    pmax x1, blocking collectives, per_device(): top = lax.pmax(jnp.max(z_final, 1), 'cols')  110 us
    all_gather x1, waiting for transfers between devices, per_device(): rows_here = lax.all_gather(noise, 'cols', axis=0, tiled=True)  64.1 us
    psum x4, blocking collectives, per_device(): col_total = lax.psum(jnp.sum(jnp.exp(z_cols - col_top[None, :]), 0), 'rows')  50.3 us
  transfers between devices with their start and end apart: 2, of which 2 were waited for; matrix products, arithmetic and copies ran while one was open for 0% of the time, Pallas kernels for 0%

commit v1 on v0

v1 whole, which is shorter than its diff:
```python
import functools
import math

import jax
import jax.numpy as jnp
from jax import lax
from jax.experimental import pallas as pl
from jax.experimental.pallas import tpu as pltpu
from jax.sharding import PartitionSpec as P

MESH = pl.DeviceIdType.MESH
F32 = jnp.float32
BF16 = jnp.bfloat16

ITERS = 4
NR = 8
NZ, NX = 8, 4
NC = NZ * NX
B = 128
D = 256
ROWS = NR * B
CHUNK = 64
SHIFT = 20.0
TO_LOG2 = 2.0 / math.log(2.0)
INV_LN2 = 1.0 / math.log(2.0)


def log2(v):
    return jnp.log(v) * INV_LN2


def wait_bytes(ref, sem):
    pltpu.make_async_copy(ref, ref, sem).wait()


def lanes_to_vector(acc_ref, b):
    return jnp.sum(acc_ref[pl.ds(b * B, B), :].T, axis=0, keepdims=True)


def spread(vec):
    return jnp.broadcast_to(vec, (B, B)).T


def kernel(
    noise, data, out,
    tile, dfull, nfull, top, acc, vec, uwide, colw, colv, colc, colm,
    rsrc, rdst, xsrc, xdst, zsrc, zdst, wts, num, den, numr, denr,
    own_sem, nsem, dsend, drecv, rsem, xsem, zsem, fsem,
):
    r = lax.axis_index("rows")
    c = lax.axis_index("cols")
    z = c // NX
    x = lax.rem(c, NX)

    def row_peer(k):
        return (lax.rem(r + k, NR), c)

    def x_peer(k):
        return (r, z * NX + lax.rem(x + k, NX))

    def z_peer(k):
        return (r, lax.rem(z + k, NZ) * NX + x)

    barrier = pltpu.get_barrier_semaphore()
    peers = [row_peer(k) for k in range(1, NR)]
    peers += [x_peer(k) for k in range(1, NX)] + [z_peer(k) for k in range(1, NZ)]
    for peer in peers:
        pl.semaphore_signal(barrier, inc=1, device_id=peer, device_id_type=MESH)
    pl.semaphore_wait(barrier, len(peers))

    def remote(src, dst, send, recv, peer):
        return pltpu.make_async_remote_copy(
            src_ref=src, dst_ref=dst, send_sem=send, recv_sem=recv, device_id=peer, device_id_type=MESH
        )

    def pass_on(block, k):
        remote(dfull.at[block], dfull.at[block], dsend, drecv.at[block], z_peer(k)).start()

    def source(dz, dx):
        return lax.rem(z + dz + NZ, NZ) * NX + lax.rem(x + dx + NX, NX)

    own_d = pltpu.make_async_copy(data, dfull.at[c], own_sem.at[0])
    own_d.start()
    for k in (1, NZ - 1):
        remote(data, dfull.at[c], dsend, drecv.at[c], z_peer(k)).start()
    for k in range(1, NX):
        remote(data, dfull.at[c], dsend, drecv.at[c], x_peer(k)).start()
    own_n = pltpu.make_async_copy(noise, nfull.at[r], own_sem.at[1])
    own_n.start()
    for k in range(1, NR):
        remote(noise, nfull.at[r], nsem.at[0], nsem.at[1], row_peer(k)).start()

    top[...] = jnp.full_like(top, -1e30)
    acc[...] = jnp.zeros_like(acc)

    def add_set(dz):
        base = pl.multiple_of(lax.rem(z + dz + NZ, NZ) * NX, NX)
        right = dfull[pl.ds(base, NX)].reshape(NX * B, D)

        def rows_step(i, carry):
            left = nfull[pl.ds(2 * i, 2)].reshape(2 * B, D)
            s = lax.dot_general(left, right, (((1,), (1,)), ((), ())), preferred_element_type=F32)
            s = s * (D ** -0.5 * TO_LOG2)
            rows = pl.ds(pl.multiple_of(i * 2 * B, 2 * B), 2 * B)
            for j in range(NX):
                tile[base + j, rows, :] = s[:, j * B:(j + 1) * B]
            return carry

        lax.fori_loop(0, NR // 2, rows_step, 0)

        def lse_step(i, carry):
            rows = pl.ds(pl.multiple_of(i * CHUNK, CHUNK), CHUNK)
            s = [tile[base + j, rows, :] for j in range(NX)]
            old = top[rows, :]
            new = jnp.maximum(old, jnp.maximum(jnp.maximum(s[0], s[1]), jnp.maximum(s[2], s[3])))
            total = acc[rows, :] * jnp.exp2(old - new)
            for j in range(NX):
                total = total + jnp.exp2(s[j] - new)
            top[rows, :] = new
            acc[rows, :] = total
            return carry

        lax.fori_loop(0, ROWS // CHUNK, lse_step, 0)

    for dx in range(1, NX):
        block = source(0, -dx)
        wait_bytes(dfull.at[block], drecv.at[block])
        pass_on(block, 1)
        pass_on(block, NZ - 1)
    wait_bytes(nfull.at[pl.ds(0, NR - 1)], nsem.at[1])
    own_n.wait()
    own_d.wait()
    add_set(0)
    half = NZ // 2
    for s in range(1, half):
        for dx in range(NX):
            ahead, behind = source(-s, -dx), source(s, -dx)
            wait_bytes(dfull.at[ahead], drecv.at[ahead])
            if s < half - 1 or dx < NX // 2:
                pass_on(ahead, 1)
            wait_bytes(dfull.at[behind], drecv.at[behind])
            if s < half - 1 or dx >= NX // 2:
                pass_on(behind, NZ - 1)
        add_set(-s)
        add_set(s)
    for dx in range(NX):
        block = source(half, -dx)
        wait_bytes(dfull.at[block], drecv.at[block])
    add_set(half)
    wait_bytes(dfull.at[pl.ds(0, NC - 1)], dsend)
    wait_bytes(nfull.at[pl.ds(0, NR - 1)], nsem.at[0])

    def exchange(src, dst, sems, group, size):
        for k in range(1, size):
            remote(src, dst.at[k - 1], sems.at[0], sems.at[1], group(k)).start()
        wait_bytes(dst, sems.at[1])
        wait_bytes(dst, sems.at[0])

    def lse(own, others, n):
        high = own
        for k in range(n):
            high = jnp.maximum(high, others[k])
        total = jnp.exp2(own - high)
        for k in range(n):
            total = total + jnp.exp2(others[k] - high)
        return high + log2(total)

    def add(own, others, n):
        for k in range(n):
            own = own + others[k]
        return own

    def finish_rows(i, carry):
        rows = pl.ds(pl.multiple_of(i * CHUNK, CHUNK), CHUNK)
        high = top[rows, :]
        row_top = jnp.max(high, axis=1, keepdims=True)
        acc[rows, :] = acc[rows, :] * jnp.exp2(high - row_top)
        top[rows, :] = jnp.broadcast_to(row_top, (CHUNK, B))
        return carry

    lax.fori_loop(0, ROWS // CHUNK, finish_rows, 0)
    for b in range(NR):
        row_top = top[pl.ds(b * B, B), :].T[0:1, :]
        rsrc[0, b:b + 1, :] = row_top + log2(lanes_to_vector(acc, b))
    exchange(rsrc.at[0], rdst.at[0], rsem.at[0], row_peer, NR)
    vec[...] = -lse(rsrc[0], rdst.at[0], NR - 1)

    def widen():
        for b in range(NR):
            uwide[pl.ds(b * B, B), :] = spread(vec[b:b + 1, :])

    widen()

    def first_cols(j, carry):
        def top_step(i, high):
            rows = pl.ds(pl.multiple_of(i * 2 * B, 2 * B), 2 * B)
            zed = tile[j, rows, :] + uwide[rows, :]
            return jnp.maximum(high, jnp.max(zed.reshape(2 * B // 8, 8, B), axis=0))

        high = lax.fori_loop(0, ROWS // (2 * B), top_step, jnp.full((8, B), -1e30, F32))
        high = jnp.max(high, axis=0, keepdims=True)

        def exp_step(i, total):
            rows = pl.ds(pl.multiple_of(i * 2 * B, 2 * B), 2 * B)
            e = jnp.exp2(tile[j, rows, :] + uwide[rows, :] - (high - SHIFT))
            tile[j, rows, :] = e
            return total + jnp.sum(e.reshape(2 * B // 8, 8, B), axis=0)

        total = lax.fori_loop(0, ROWS // (2 * B), exp_step, jnp.zeros((8, B), F32))
        colm[pl.ds(j, 1), :] = high
        colc[pl.ds(j, 1), :] = jnp.sum(total, axis=0, keepdims=True)
        return carry

    lax.fori_loop(0, NC, first_cols, 0)
    xsrc[0] = colm[...] + (log2(colc[...]) - SHIFT)
    exchange(xsrc.at[0], xdst.at[0], xsem.at[0], x_peer, NX)
    zsrc[0] = lse(xsrc[0], xdst.at[0], NX - 1)
    exchange(zsrc.at[0], zdst.at[0], zsem.at[0], z_peer, NZ)
    colw[...] = jnp.exp2(colm[...] - lse(zsrc[0], zdst.at[0], NZ - 1) + SHIFT)
    colv[...] = colw[...]

    def iteration(t, carry):
        def rows_pass(i, carry):
            rows = pl.ds(pl.multiple_of(i * CHUNK, CHUNK), CHUNK)
            total = tile[0, rows, :] * colv[0:1, :]
            for j in range(1, NC):
                total = total + tile[j, rows, :] * colv[j:j + 1, :]
            acc[rows, :] = total
            return carry

        lax.fori_loop(0, ROWS // CHUNK, rows_pass, 0)
        for b in range(NR):
            rsrc[t, b:b + 1, :] = lanes_to_vector(acc, b)
        exchange(rsrc.at[t], rdst.at[t], rsem.at[t], row_peer, NR)
        vec[...] = 1.0 / add(rsrc[t], rdst.at[t], NR - 1)
        widen()

        def cols_pass(j, carry):
            def step(i, totals):
                rows = pl.ds(pl.multiple_of(i * 2 * B, 2 * B), 2 * B)
                u = uwide[rows, :]
                return tuple(
                    total + jnp.sum((tile[4 * j + k, rows, :] * u).reshape(2 * B // 8, 8, B), axis=0)
                    for k, total in enumerate(totals)
                )

            totals = lax.fori_loop(0, ROWS // (2 * B), step, (jnp.zeros((8, B), F32),) * 4)
            for k in range(4):
                colc[pl.ds(4 * j + k, 1), :] = jnp.sum(totals[k], axis=0, keepdims=True)
            return carry

        lax.fori_loop(0, NC // 4, cols_pass, 0)
        xsrc[t] = colc[...] * colw[...]
        exchange(xsrc.at[t], xdst.at[t], xsem.at[t], x_peer, NX)
        zsrc[t] = add(xsrc[t], xdst.at[t], NX - 1)
        exchange(zsrc.at[t], zdst.at[t], zsem.at[t], z_peer, NZ)
        colv[...] = colw[...] / add(zsrc[t], zdst.at[t], NZ - 1)
        return carry

    lax.fori_loop(1, ITERS, iteration, 0)

    def weigh(q):
        def step(i, carry):
            rows = pl.ds(pl.multiple_of(q * 2 * B + i * CHUNK, CHUNK), CHUNK)
            to = pl.ds(pl.multiple_of(i * CHUNK, CHUNK), CHUNK)
            total = jnp.zeros((CHUNK, B), F32)
            for j in range(NC):
                w = (tile[j, rows, :] * colv[j:j + 1, :]).astype(BF16)
                wts[to, j * B:(j + 1) * B] = w
                total = total + w.astype(F32)
            acc[to, :] = total
            return carry

        lax.fori_loop(0, 2 * B // CHUNK, step, 0)
        n = jnp.dot(wts[...], dfull[...].reshape(NC * B, D), preferred_element_type=F32)
        num[pl.ds(2 * q, 2)] = n.reshape(2, B, D)
        for b in range(2):
            den[2 * q + b] = lanes_to_vector(acc, b)

    def send(b):
        slot = lax.rem(r - b + NR, NR) - 1
        remote(num.at[b], numr.at[slot], fsem.at[0], fsem.at[1], (b, c)).start()
        remote(den.at[b], denr.at[slot], fsem.at[2], fsem.at[3], (b, c)).start()

    mine = r // 2

    def final(i, carry):
        q = lax.rem(mine + i, NR // 2)
        weigh(q)
        send(2 * q)
        send(2 * q + 1)
        return carry

    lax.fori_loop(1, NR // 2, final, 0)
    weigh(mine)
    send(2 * mine + 1 - lax.rem(r, 2))
    wait_bytes(numr, fsem.at[1])
    wait_bytes(denr, fsem.at[3])
    total = num[r]
    weight = den[r]
    for k in range(NR - 1):
        total = total + numr[k]
        weight = weight + denr[k]
    scale = spread(weight)
    out[:, 0:B] = total[:, 0:B] / scale
    out[:, B:D] = total[:, B:D] / scale
    wait_bytes(numr, fsem.at[0])
    wait_bytes(denr, fsem.at[2])


def solution(mesh):
    vmem, dma = pltpu.VMEM, pltpu.SemaphoreType.DMA
    scratch = [
        vmem((NC, ROWS, B), F32),
        vmem((NC, B, D), BF16),
        vmem((NR, B, D), BF16),
        vmem((ROWS, B), F32),
        vmem((ROWS, B), F32),
        vmem((NR, B), F32),
        vmem((ROWS, B), F32),
        vmem((NC, B), F32),
        vmem((NC, B), F32),
        vmem((NC, B), F32),
        vmem((NC, B), F32),
        vmem((ITERS, NR, B), F32),
        vmem((ITERS, NR - 1, NR, B), F32),
        vmem((ITERS, NC, B), F32),
        vmem((ITERS, NX - 1, NC, B), F32),
        vmem((ITERS, NC, B), F32),
        vmem((ITERS, NZ - 1, NC, B), F32),
        vmem((2 * B, NC * B), BF16),
        vmem((NR, B, D), F32),
        vmem((NR, 1, B), F32),
        vmem((NR - 1, B, D), F32),
        vmem((NR - 1, 1, B), F32),
        dma((2,)),
        dma((2,)),
        dma,
        dma((NC,)),
        dma((ITERS, 2)),
        dma((ITERS, 2)),
        dma((ITERS, 2)),
        dma((4,)),
    ]

    def per_device(noise, data):
        return pl.pallas_call(
            kernel,
            out_shape=jax.ShapeDtypeStruct((B, D), F32),
            in_specs=[pl.BlockSpec(memory_space=pltpu.VMEM)] * 2,
            out_specs=pl.BlockSpec(memory_space=pltpu.VMEM),
            scratch_shapes=scratch,
            compiler_params=pltpu.CompilerParams(
                collective_id=0, has_side_effects=True, vmem_limit_bytes=40 << 20
            ),
        )(noise, data)

    return jax.shard_map(
        per_device,
        mesh=mesh,
        in_specs=(P(("rows", "cols"), None), P(("cols", "rows"), None)),
        out_specs=P(("rows", "cols"), None),
        check_vma=False,
    )
```

time: 1820 us -> 129 us (0.07)
  blocking collectives: 1440 us -> 0 us
  waiting for transfers between devices: 192 us -> 0 us
  other arithmetic: 139 us -> 0 us
  Pallas kernels: 0 us -> 127 us
    pmax x9 -> x0, blocking collectives: 826 us -> none  [the longest x4 442 us: per_device(): top = lax.pmax(jnp.max(z_rows, 1), 'cols')]
    psum x8 -> x0, blocking collectives: 492 us -> none  [the longest x4 442 us: per_device(): total = lax.psum(jnp.sum(jnp.exp(z_rows - top[:, None]), 1), 'cols')]
    reduce_scatter x1 -> x0, waiting for transfers between devices: 127 us -> none  [per_device(): lax.psum_scatter(numerator, 'cols', scatter_dimension=0, tiled=True)]
    pallas_call x0 -> x1, Pallas kernels: none -> 127 us  [per_device(): pl.pallas_call(kernel, out_shape=jax.ShapeDtypeStruct((B, D), F32), in_sp...]
    unnamed x1 -> x0, blocking collectives: 110 us -> none
    reduce_sum x9 -> x0, other arithmetic: 73.1 us -> none  [the longest x4 32.5 us: per_device(): total = lax.psum(jnp.sum(jnp.exp(z_rows - top[:, None]), 1), 'cols')]
    reduce_max x8 -> x0, other arithmetic: 64.7 us -> none  [the longest x4 32 us: per_device(): col_top = lax.pmax(jnp.max(z_cols, 0), 'rows')]
    all_gather x1 -> x0, waiting for transfers between devices: 64.1 us -> none  [per_device(): rows_here = lax.all_gather(noise, 'cols', axis=0, tiled=True)]
  transfers between devices with their start and end apart: 2 -> 0, of which waited for: 2 -> 0; matrix products, arithmetic and copies ran while one was open for 0% -> 0% of each run, Pallas kernels for 0% -> 0%
where the time goes in v1:
time: 129 us
  Pallas kernels  127 us (98%)
  local copies, waits for them, and re-layouts  2.34 us (2%)
    pallas_call x1, Pallas kernels, per_device(): pl.pallas_call(kernel, out_shape=jax.ShapeDtypeStruct((B, D), F32), in_sp...  127 us

profile of v1, /device:TPU:1, one launch (start us, length us, event | category | flops | bytes accessed | tf_op | source)
XLA Modules:
  0.0 129.2 jit_solution(15790291596260118879)
XLA Ops:
  0.0 0.0 copy-start
  0.0 0.8 copy-done
  0.8 0.0 copy-start.1
  0.8 0.8 copy-done.1
  1.7 126.9 %shard_map.28 = f32[128,256]{1,0:T(8,128)S(1)} custom-call(bf16[128,256]{1,0:T(8,128)(2,1)S(1)} %copy-done, bf16[128,256]{1,0:T(8,128)(2,1)S(1)} %copy-done.1), custom_call_target="tpu_custom_call" | custom-call | tf_op jit(solution)/shard_map/pallas_call | solution.py:347
  128.6 0.7 copy.4
Async XLA Ops:
  0.0 0.8 copy-start
  0.8 0.8 copy-start.1
